TPU v7x, 256 devices: a whole 4x4x8 slice. The times are simulated.
256 devices in a mesh: inst: 32 (over x, y, core), tp: 8 (over z).
Axes of the slice: x: 4, y: 4, z: 8, core: 2. Of those that a mesh axis runs over, the one named last changes fastest.
Arguments:
- queries: bfloat16 [1024, 64, 128], P('inst', 'tp'), may hold values from -100 to 100
- new_keys: bfloat16 [1024, 8, 128], P('inst', 'tp'), may hold values from -4 to 4
- new_values: bfloat16 [1024, 8, 128], P('inst', 'tp'), may hold values from -6 to 6
- cache_keys: bfloat16 [16384, 16, 8, 128], P('inst', None, 'tp'), may hold values from -4 to 4
- cache_values: bfloat16 [16384, 16, 8, 128], P('inst', None, 'tp'), may hold values from -6 to 6
- page_table: int32 [1024, 32], P('inst'), may hold values from 0 to 511, as said below
- lengths: int32 [1024], P('inst'), may hold values from 1 to 512, 262144 in all
- remote_keys: bfloat16 [32768, 16, 8, 128], P('inst', None, 'tp'), may hold values from -4 to 4
- remote_values: bfloat16 [32768, 16, 8, 128], P('inst', None, 'tp'), may hold values from -6 to 6
- counts: int32 [32, 32], P('inst'), may hold values from 0 to 32, as said below
- page_owner: int32 [32, 32, 32], P('inst'), may hold values from 0 to 3
- query_list: int32 [32, 32, 4], P('inst'), may hold values from 0 to 31
Outputs:
- attended: bfloat16 [1024, 64, 128], P('inst', 'tp')
Inputs may be any that keep to these rules, and one draw needn't show every extreme that they name: Within one instance, the first pages page_table[r, 0] of its 32 requests are distinct; other entries may repeat. `counts`: one helper, drawn from the seed, stores 32 pages for every owner instance.
All inputs are finite; a program needn't handle non-finite values. No bound on the sum of `lengths` on one device may be relied on, other than what follows from the above.
Results may differ from a plain program's by a relative error of at most 0.022.
Values may be sent and summed in bfloat16 or wider, within the bound.
A program may use at most 128 MiB of HBM per device.

v0:
```python
import jax
import jax.numpy as jnp
from jax import lax
from jax.sharding import PartitionSpec as P


def partial_softmax(scores, allowed):
    masked = jnp.where(allowed, scores, -1e30)
    highest = jnp.max(masked, axis=-1)
    weights = jnp.where(allowed, jnp.exp(scores - highest[..., None]), 0.0)
    return (highest, jnp.sum(weights, axis=-1), weights.astype(jnp.bfloat16))


def combine_parts(first, second):
    first_peak, first_sum, first_out = first
    second_peak, second_sum, second_out = second
    joint_peak = jnp.maximum(first_peak, second_peak)
    first_factor = jnp.exp(first_peak - joint_peak)
    second_factor = jnp.exp(second_peak - joint_peak)
    joint_sum = first_sum * first_factor + second_sum * second_factor
    joint_out = first_out * first_factor[..., None] + second_out * second_factor[..., None]
    return (joint_peak, joint_sum, joint_out)


def fold_slots(running, slot_lists, back_peak, back_sum, back_out, requests):
    slot_total = slot_lists.shape[0] * slot_lists.shape[1]
    key_heads, group_size, head_dim = (back_out.shape[-3], back_out.shape[-2], back_out.shape[-1])
    back_peak = back_peak.reshape(slot_total, key_heads, group_size)
    back_sum = back_sum.reshape(slot_total, key_heads, group_size)
    back_out = back_out.reshape(slot_total, key_heads, group_size, head_dim)
    slot_match = (
        slot_lists.reshape(slot_total)[:, None] == jnp.arange(requests, dtype=jnp.int32)[None, :]
    )
    slot_onehot = slot_match.astype(jnp.float32)
    current_peak, current_sum, current_out = running
    slot_top = jnp.max(jnp.where(slot_match[:, :, None, None], back_peak[:, None], -1e30), axis=0)
    row_peak = jnp.maximum(current_peak, slot_top)
    slot_peak = jnp.einsum("sr,rkg->skg", slot_onehot, row_peak, precision=lax.Precision.HIGHEST)
    factor = jnp.exp(back_peak - slot_peak)
    rescale = jnp.exp(current_peak - row_peak)
    joint_sum = current_sum * rescale + jnp.einsum(
        "sr,skg->rkg", slot_onehot, back_sum * factor, precision=lax.Precision.HIGHEST
    )
    joint_out = current_out * rescale[..., None] + jnp.einsum(
        "sr,skgd->rkgd", slot_onehot, back_out * factor[..., None], precision=lax.Precision.HIGHEST
    )
    return (row_peak, joint_sum, joint_out)


def per_device(
    queries,
    new_keys,
    new_values,
    cache_keys,
    cache_values,
    page_table,
    lengths,
    remote_keys,
    remote_values,
    counts,
    page_owner,
    query_list,
):
    requests, query_heads, head_dim = queries.shape
    key_heads = new_keys.shape[1]
    group_size = query_heads // key_heads
    page_count = page_table.shape[1]
    page_length = cache_keys.shape[1]
    helpers = lax.axis_size("inst")
    capacity = remote_keys.shape[0] // helpers
    slot_count = query_list.shape[2]
    score_scale = head_dim ** (-0.5)
    grouped = queries.reshape(requests, key_heads, group_size, head_dim)
    local_keys = cache_keys[page_table].reshape(
        requests, page_count * page_length, key_heads, head_dim
    )
    local_values = cache_values[page_table].reshape(
        requests, page_count * page_length, key_heads, head_dim
    )
    live_tokens = jnp.arange(page_count * page_length, dtype=jnp.int32)[None, :] < lengths[:, None]
    local_scores = (
        jnp.einsum("rkgd,rtkd->rkgt", grouped, local_keys, preferred_element_type=jnp.float32)
        * score_scale
    )
    local_peak, local_sum, local_weights = partial_softmax(
        local_scores, live_tokens[:, None, None, :]
    )
    local_out = jnp.einsum(
        "rkgt,rtkd->rkgd", local_weights, local_values, preferred_element_type=jnp.float32
    )
    new_scores = (
        jnp.einsum("rkgd,rkd->rkg", grouped, new_keys, preferred_element_type=jnp.float32)
        * score_scale
    )
    new_out = jnp.broadcast_to(new_values[:, :, None, :].astype(jnp.float32), local_out.shape)
    running = combine_parts(
        (local_peak, local_sum, local_out), (new_scores, jnp.ones_like(new_scores), new_out)
    )
    filled_slot = jnp.arange(capacity, dtype=jnp.int32)[None, :] < counts[0][:, None]
    owner_match = (
        page_owner[0][:, :, None] == jnp.arange(slot_count, dtype=jnp.int32)[None, None, :]
    ) & filled_slot[:, :, None]
    slot_lists = query_list[0]
    page_block = (helpers, capacity, page_length, key_heads, head_dim)
    home_keys, home_values, home_owner = (
        lax.all_to_all(
            remote_keys.reshape(page_block), "inst", split_axis=0, concat_axis=0, tiled=True
        ),
        lax.all_to_all(
            remote_values.reshape(page_block), "inst", split_axis=0, concat_axis=0, tiled=True
        ),
        lax.all_to_all(
            owner_match.astype(jnp.bfloat16), "inst", split_axis=0, concat_axis=0, tiled=True
        ),
    )
    slot_queries = grouped[slot_lists]
    slot_pages = jnp.swapaxes(home_owner, 1, 2) > 0.5
    token_mask = jnp.broadcast_to(
        slot_pages[:, :, :, None], (helpers, slot_count, capacity, page_length)
    ).reshape(helpers, slot_count, capacity * page_length)
    near_keys = home_keys.reshape(helpers, capacity * page_length, key_heads, head_dim)
    near_values = home_values.reshape(helpers, capacity * page_length, key_heads, head_dim)
    slot_scores = (
        jnp.einsum("aqkgd,atkd->aqkgt", slot_queries, near_keys, preferred_element_type=jnp.float32)
        * score_scale
    )
    slot_peak, slot_sum, slot_weights = partial_softmax(
        slot_scores, token_mask[:, :, None, None, :]
    )
    slot_out = jnp.einsum(
        "aqkgt,atkd->aqkgd", slot_weights, near_values, preferred_element_type=jnp.float32
    )
    running = fold_slots(running, slot_lists, slot_peak, slot_sum, slot_out, requests)
    final_peak, final_sum, final_out = running
    return (
        (final_out / final_sum[..., None])
        .astype(jnp.bfloat16)
        .reshape(requests, query_heads, head_dim)
    )


def solution(mesh):
    return jax.shard_map(
        per_device,
        mesh=mesh,
        in_specs=(
            P("inst", "tp", None),
            P("inst", "tp", None),
            P("inst", "tp", None),
            P("inst", None, "tp", None),
            P("inst", None, "tp", None),
            P("inst", None),
            P("inst"),
            P("inst", None, "tp", None),
            P("inst", None, "tp", None),
            P("inst", None),
            P("inst", None, None),
            P("inst", None, None),
        ),
        out_specs=P("inst", "tp", None),
        check_vma=False,
    )
```

profile of v0, /device:TPU:1, one launch (start us, length us, event | category | flops | bytes accessed | tf_op | source)
XLA Modules:
  0.0 135.5 jit_solution(1222267736553026127)
XLA Ops:
  0.0 0.9 iota_compare_fusion.2
  0.9 0.8 fusion.24
  1.6 15.7 %all_to_all.15 = bf16[32,32,4]{1,2,0:T(4,128)(2,1)S(1)} all-to-all(bf16[32,32,4]{1,2,0:T(4,128)(2,1)S(1)} %fusion.24), channel_id=1, replica_groups=mesh['inst'=32,'tp'=8] {'inst'}, dimensions={0} | all-to-all | bytes 16384 | tf_op jit(solution)/shard_map/all_to_all | solution.py:112
  17.3 55.6 %all_to_all.16 = bf16[32,32,16,1,128]{4,2,1,3,0:T(8,128)(2,1)} all-to-all(bf16[32,32,16,1,128]{4,2,1,3,0:T(8,128)(2,1)} %bitcast.97), channel_id=1, replica_groups=mesh['inst'=32,'tp'=8] {'inst'}, dimensions={0} | all-to-all | bytes 8388608 | tf_op jit(solution)/shard_map/all_to_all | solution.py:106
  72.9 4.8 %all-to-all-start.2 = ((bf16[32,32,16,1,128]{4,2,1,3,0:T(8,128)(2,1)}), bf16[32,32,16,1,128]{4,2,1,3,0:T(8,128)(2,1)}, u32[]{:S(2)}, u32[]{:S(2)}) async-start(bf16[32,32,16,1,128]{4,2,1,3,0:T(8,128)(2,1)} %bitcast.98), calls=%async_computation.2 | async-start | bytes 8388608 | tf_op jit(solution)/shard_map/all_to_all | solution.py:109
  77.9 0.1 reshape.304
  78.0 0.1 eq.34
  78.2 0.7 gather_fusion.2
  78.9 8.5 %gather_fusion = bf16[1024,16,128]{2,1,0:T(8,128)(2,1)} fusion(bf16[512,16,128]{2,1,0:T(8,128)(2,1)S(1)} %bitcast.92, s32[1024]{0:T(1024)S(1)} %broadcast_clamp_fusion), kind=kCustom, calls=%fused_computation | custom fusion | bytes 8392704 | tf_op jit(solution)/shard_map/gather | solution.py:74
  87.5 3.5 %select_reduce_fusion = (f32[32,8]{1,0:T(8,128)S(1)}, f32[32,512,8]{1,2,0:T(8,128)S(1)}) fusion(pred[32,512]{1,0:T(8,128)(4,1)S(1)} %iota_compare_fusion.1, bf16[32,512,128]{2,1,0:T(8,128)(2,1)} %bitcast.95, bf16[32,8,128]{2,1,0:T(8,128)(2,1)S(1)} %copy-done.2), kind=kOutput, calls=%fused_computation.31 | convolution fusion | flops 33947392 | bytes 4801536 | tf_op jit(solution)/shard_map/rkgd,rtkd->rkgt/dot_general | solution.py:82
  91.0 0.2 fusion.25
  91.2 0.3 bitcast_reduce_fusion
  91.6 10.1 %gather_fusion.1 = bf16[1024,16,128]{2,1,0:T(8,128)(2,1)} fusion(bf16[512,16,128]{2,1,0:T(8,128)(2,1)} %bitcast.96, s32[1024]{0:T(1024)S(1)} %broadcast_clamp_fusion), kind=kCustom, calls=%fused_computation.1 | custom fusion | bytes 8392704 | tf_op jit(solution)/shard_map/gather | solution.py:77
  101.7 0.1 copy.60
  101.9 0.3 copy.61
  102.3 5.0 %fusion = (f32[32,4,8]{2,1,0:T(4,128)S(1)}, f32[32,4,8,512]{3,2,1,0:T(8,128)}) fusion(pred[32,4,512]{2,1,0:T(4,128)(4,1)S(1)} %copy.61, bf16[32,4,8,128]{3,2,1,0:T(8,128)(2,1)S(1)} %bitcast.101, bf16[32,512,128,1]{2,1,3,0:T(8,128)(2,1)} %bitcast.94), kind=kOutput, calls=%fused_computation.5 | convolution fusion | flops 135789568 | bytes 6623232 | tf_op jit(solution)/shard_map/aqkgd,atkd->aqkgt/dot_general | solution.py:124
  107.4 0.1 select_reduce_fusion.1
  107.6 2.4 %fusion.3 = f32[32,4,8]{2,1,0:T(4,128)S(1)} fusion(f32[32,4,8,512]{3,2,1,0:T(8,128)} %get-tuple-element.11, f32[32,4,8]{2,1,0:T(4,128)S(1)} %get-tuple-element.10, pred[32,4,512]{2,1,0:T(4,128)(4,1)S(1)} %copy.61), kind=kLoop, calls=%fused_computation.8 | loop fusion | flops 2096128 | bytes 2170880 | tf_op jit(solution)/shard_map/reduce_sum | solution.py:11
  110.2 0.1 fusion.10
  110.4 0.1 convolution_add_fusion
  110.6 19.3 %all-to-all-done.2 = bf16[32,32,16,1,128]{4,2,1,3,0:T(8,128)(2,1)} async-done(((bf16[32,32,16,1,128]{4,2,1,3,0:T(8,128)(2,1)}), bf16[32,32,16,1,128]{4,2,1,3,0:T(8,128)(2,1)}, u32[]{:S(2)}, u32[]{:S(2)}) %all-to-all-start.2) | async-done | bytes 4194336 | tf_op jit(solution)/shard_map/all_to_all | solution.py:109
  129.9 3.7 %fusion.12 = f32[32,4,8,128]{3,2,1,0:T(8,128)S(1)} fusion(bf16[32,512,128,1]{2,1,3,0:T(8,128)(2,1)} %bitcast.30, f32[32,4,8,512]{3,2,1,0:T(8,128)} %get-tuple-element.11, f32[32,4,8]{2,1,0:T(4,128)S(1)} %get-tuple-element.10, pred[32,4,512]{2,1,0:T(4,128)(4,1)S(1)} %copy.61), kind=kOutput, calls=%fused_computation.21 | convolution fusion | flops 136314880 | bytes 6885376 | tf_op jit(solution)/shard_map/aqkgt,atkd->aqkgd/dot_general | solution.py:130
  133.6 0.4 fusion.18
  134.0 1.5 %fusion.9 = bf16[32,8,128]{2,1,0:T(8,128)(2,1)} fusion(bf16[32,512,128]{2,1,0:T(8,128)(2,1)S(1)} %bitcast.93, f32[32,512,8]{1,2,0:T(8,128)S(1)} %get-tuple-element.9, f32[32,8]{1,0:T(8,128)S(1)} %get-tuple-element.8, pred[32,512]{1,0:T(8,128)(4,1)S(1)} %iota_compare_fusion.1, f32[32,8,128]{2,0,1:T(8,128)S(1)} %fusion.18, f32[32,8]{1,0:T(8,128)S(1)} %copy.71, ...), kind=kOutput, calls=%fused_computation.16 | convolution fusion | flops 34177024 | bytes 4953088 | tf_op jit(solution)/shard_map/rkgt,rtkd->rkgd/dot_general | solution.py:88
  (39 shorter events, 1.2 us)
Async XLA Ops:
  0.0 78.9 %copy-start = (bf16[512,16,1,128]{3,1,2,0:T(8,128)(2,1)S(1)}, bf16[512,16,1,128]{3,1,2,0:T(8,128)(2,1)}, u32[]{:S(2)}) copy-start(bf16[512,16,1,128]{3,1,2,0:T(8,128)(2,1)} %param.15) | copy-start | bytes 6291460
  72.9 4.8 %copy-start.5 = (s32[1,32,4]{1,2,0:T(4,128)S(1)}, s32[1,32,4]{1,2,0:T(4,128)}, u32[]{:S(2)}) copy-start(s32[1,32,4]{1,2,0:T(4,128)} %param.23) | copy-start | bytes 1540
  72.9 5.2 %copy-start.3 = (s32[32,32]{1,0:T(8,128)S(1)}, s32[32,32]{1,0:T(8,128)}, u32[]{:S(2)}) copy-start(s32[32,32]{1,0:T(8,128)} %param.17) | copy-start | bytes 12292
  72.9 5.3 %copy-start.2 = (bf16[32,8,128]{2,1,0:T(8,128)(2,1)S(1)}, bf16[32,8,128]{2,1,0:T(8,128)(2,1)}, u32[]{:S(2)}) copy-start(bf16[32,8,128]{2,1,0:T(8,128)(2,1)} %param.12) | copy-start | bytes 196612
  72.9 57.0 %all-to-all-start.2 = ((bf16[32,32,16,1,128]{4,2,1,3,0:T(8,128)(2,1)}), bf16[32,32,16,1,128]{4,2,1,3,0:T(8,128)(2,1)}, u32[]{:S(2)}, u32[]{:S(2)}) async-start(bf16[32,32,16,1,128]{4,2,1,3,0:T(8,128)(2,1)} %bitcast.98), calls=%async_computation.2 | async-start | bytes 8388608 | tf_op jit(solution)/shard_map/all_to_all | solution.py:109
  78.9 8.5 %copy-start.6 = (s32[32]{0:T(128)S(1)}, s32[32]{0:T(128)}, u32[]{:S(2)}) copy-start(s32[32]{0:T(128)} %param.18) | copy-start | bytes 388
  87.5 3.5 %copy-start.7 = (bf16[32,1,128]{2,0,1:T(8,128)(2,1)S(1)}, bf16[32,1,128]{2,0,1:T(8,128)(2,1)}, u32[]{:S(2)}) copy-start(bf16[32,1,128]{2,0,1:T(8,128)(2,1)} %param.13) | copy-start | bytes 24580
  91.6 10.1 %copy-start.4 = (bf16[32,1,128]{2,0,1:T(8,128)(2,1)S(1)}, bf16[32,1,128]{2,0,1:T(8,128)(2,1)}, u32[]{:S(2)}) copy-start(bf16[32,1,128]{2,0,1:T(8,128)(2,1)} %param.14) | copy-start | bytes 24580
  129.9 4.2 %copy-start.1 = (bf16[1024,16,128]{2,1,0:T(8,128)(2,1)S(1)}, bf16[1024,16,128]{2,1,0:T(8,128)(2,1)}, u32[]{:S(2)}) copy-start(bf16[1024,16,128]{2,1,0:T(8,128)(2,1)} %gather_fusion.1) | copy-start | bytes 12582916
where the time goes:
time: 137 us; the launch traced here: 135 us
  blocking collectives  71.2 us (52%)
  local copies, waits for them, and re-layouts  21 us (15%)
  waiting for transfers between devices  19.3 us (14%)
  matrix products  14.5 us (11%)
  starting transfers between devices  4.79 us (3%)
  other arithmetic  4.55 us (3%)
    all_to_all x1, blocking collectives, per_device(): lax.all_to_all(remote_keys.reshape(page_block), 'inst', split_axis=0, con...  55.6 us
    all_to_all x1, waiting for transfers between devices, per_device(): lax.all_to_all(remote_values.reshape(page_block), 'inst', split_axis=0, c...  19.3 us
    all_to_all x1, blocking collectives, per_device(): lax.all_to_all(owner_match.astype(jnp.bfloat16), 'inst', split_axis=0, co...  15.7 us
    gather x1, local copies, waits for them, and re-layouts, per_device(): cache_values[page_table]  10.1 us
    gather x1, local copies, waits for them, and re-layouts, per_device(): cache_keys[page_table]  8.48 us
    dot_general x1, matrix products, per_device(): jnp.einsum('aqkgd,atkd->aqkgt', slot_queries, near_keys, preferred_elemen...  5.03 us
    all_to_all x1, starting transfers between devices, per_device(): lax.all_to_all(remote_values.reshape(page_block), 'inst', split_axis=0, c...  4.79 us
    dot_general x1, matrix products, per_device(): jnp.einsum('aqkgt,atkd->aqkgd', slot_weights, near_values, preferred_elem...  3.71 us
  transfers between devices with their start and end apart: 1, of which 1 were waited for; matrix products, arithmetic and copies ran while one was open for 24% of the time, Pallas kernels for 0%

commit v1 on v0

v1 whole, which is shorter than its diff:
```python
import functools
import math

import jax
import jax.numpy as jnp
from jax import lax
from jax.experimental import pallas as pl
from jax.experimental.pallas import tpu as pltpu
from jax.sharding import PartitionSpec as P

MASKED = -1e30
GROUP = 8
BLOCK = 4
EARLY = 4
STATS = 16
MESH = pl.DeviceIdType.MESH


def dot_rows(a, b):
    return lax.dot_general(a, b, (((1,), (1,)), ((), ())), preferred_element_type=jnp.float32)


def dot_plain(a, b):
    return jnp.dot(a, b, preferred_element_type=jnp.float32)


def softmax_rows(scores):
    peak = jnp.max(scores, axis=1, keepdims=True)
    weights = jnp.exp2(scores - peak)
    total = jnp.sum(weights, axis=1, keepdims=True)
    return weights.astype(jnp.bfloat16), peak + jnp.log2(total), 1.0 / total


def kernel(
    table,
    lengths,
    lists,
    counts,
    owners,
    q_hbm,
    fresh_k,
    fresh_v,
    pool_k_hbm,
    pool_v_hbm,
    store_k_hbm,
    store_v_hbm,
    out,
    q,
    q_wide,
    pool_k,
    pool_v,
    store_k,
    store_v,
    ask_out,
    ask_in,
    reply_out,
    reply_in,
    slot_of,
    row_of,
    local_out,
    local_lse,
    in_sem,
    store_sem,
    ask_send,
    ask_recv,
    reply_send,
    reply_recv,
):
    requests, _, head_dim = q_wide.shape
    group = q_wide.shape[1]
    rows = requests * group
    slots, helpers = lists.shape
    slot_rows = slots * group
    pages, page = table.shape[1], pool_k.shape[1]
    tokens = pages * page
    capacity = owners.shape[1]
    groups = helpers // GROUP
    factor = math.log2(math.e) / math.sqrt(head_dim)
    me = lax.axis_index("inst")
    mine = lax.div(me, GROUP)

    barrier = pltpu.get_barrier_semaphore()

    def greet(step, _):
        pl.semaphore_signal(
            barrier,
            inc=1,
            device_id={"inst": lax.rem(me + step, helpers)},
            device_id_type=MESH,
        )
        return 0

    q_copy = pltpu.make_async_copy(q_hbm, q, in_sem.at[0])
    q_copy.start()
    lax.fori_loop(1, helpers, greet, 0)
    pool_copies = (
        pltpu.make_async_copy(pool_k_hbm, pool_k, in_sem.at[1]),
        pltpu.make_async_copy(pool_v_hbm, pool_v, in_sem.at[2]),
    )
    for copy in pool_copies:
        copy.start()

    def store_copies(step):
        first = lax.rem(mine + step, groups) * GROUP
        span = pl.ds(first, GROUP)
        return (
            pltpu.make_async_copy(store_k_hbm.at[span], store_k.at[span], store_sem.at[0, step]),
            pltpu.make_async_copy(store_v_hbm.at[span], store_v.at[span], store_sem.at[1, step]),
        )

    for step in range(groups):
        for copy in store_copies(step):
            copy.start()

    square = (helpers, helpers)
    on_diagonal = lax.broadcasted_iota(jnp.int32, square, 0) == lax.broadcasted_iota(
        jnp.int32, square, 1
    )
    filled = jnp.where(on_diagonal, jnp.broadcast_to(counts[...], square), 0).astype(jnp.float32)
    filled = jnp.sum(filled, axis=1, keepdims=True)
    column = lax.broadcasted_iota(jnp.int32, (helpers, capacity), 1).astype(jnp.float32)
    page_slot = jnp.where(column < filled, owners[...].astype(jnp.float32), -1.0)
    spread = (
        lax.div(lax.broadcasted_iota(jnp.int32, (capacity, tokens), 1), page)
        == lax.broadcasted_iota(jnp.int32, (capacity, tokens), 0)
    ).astype(jnp.float32)
    slot_of[...] = dot_plain(page_slot.astype(jnp.bfloat16), spread.astype(jnp.bfloat16))

    lane = lax.broadcasted_iota(jnp.int32, (1, 128), 1)
    packed = 128 // slot_rows
    for part in range(helpers // packed):
        line = lax.rem(lane, group)
        for piece in range(packed * slots):
            helper, slot = part * packed + piece // slots, piece % slots
            line = jnp.where(
                lax.div(lane, group) == piece, line + lists[slot, helper] * group, line
            )
        row_of[pl.ds(part, 1), :] = line

    q_copy.wait()
    q_wide[...] = q[...].astype(jnp.float32).reshape(q_wide.shape)

    def gather(helper, _):
        picked = [q_wide[lists[slot, helper]] for slot in range(slots)]
        ask_out[helper] = jnp.concatenate(picked, axis=0).astype(jnp.bfloat16)
        return 0

    lax.fori_loop(0, helpers, gather, 0)
    ask_in[me] = ask_out[me]
    pl.semaphore_wait(barrier, helpers - 1)

    def ask(target, source):
        return pltpu.make_async_remote_copy(
            src_ref=ask_out.at[target],
            dst_ref=ask_in.at[source],
            send_sem=ask_send.at[target],
            recv_sem=ask_recv.at[source],
            device_id={"inst": target},
            device_id_type=MESH,
        )

    def reply(target, source):
        return pltpu.make_async_remote_copy(
            src_ref=reply_out.at[target],
            dst_ref=reply_in.at[source],
            send_sem=reply_send.at[target],
            recv_sem=reply_recv.at[source],
            device_id={"inst": target},
            device_id_type=MESH,
        )

    def send_ask(step, _):
        first = lax.rem(mine + groups - lax.div(step, GROUP), groups) * GROUP
        target = first + lax.rem(step, GROUP)

        @pl.when(target != me)
        def _():
            ask(target, me).start()

        return 0

    lax.fori_loop(0, helpers, send_ask, 0)

    for copy in pool_copies:
        copy.wait()
    token = lax.broadcasted_iota(jnp.int32, (group, tokens), 1)

    def local_block(block, _):
        def pages_of(pool, request):
            return jnp.concatenate([pool[table[request, j]] for j in range(pages)], axis=0)

        scores = []
        for pair in range(BLOCK // 2):
            start = pl.multiple_of(block * (BLOCK * group) + pair * 2 * group, 2 * group)
            two = q[pl.ds(start, 2 * group), :]
            for side in range(2):
                request = block * BLOCK + 2 * pair + side
                both = dot_rows(two, pages_of(pool_k, request))
                one = both[side * group : (side + 1) * group]
                scores.append(jnp.where(token < lengths[request], one * factor, MASKED))
        weights, lse, inverse = softmax_rows(jnp.concatenate(scores, axis=0))
        mixed = []
        for pair in range(BLOCK // 2):
            two = weights[pair * 2 * group : (pair + 1) * 2 * group]
            for side in range(2):
                request = block * BLOCK + 2 * pair + side
                both = dot_plain(two, pages_of(pool_v, request))
                mixed.append(both[side * group : (side + 1) * group])
        start = pl.multiple_of(block * (BLOCK * group), BLOCK * group)
        span = pl.ds(start, BLOCK * group)
        local_out[span, :] = jnp.concatenate(mixed, axis=0) * inverse
        local_lse[span, :] = jnp.broadcast_to(lse, (BLOCK * group, head_dim))
        return 0

    lax.fori_loop(0, EARLY, local_block, 0)

    wide = (slot_rows, head_dim)
    row = lax.broadcasted_iota(jnp.int32, wide, 0)
    placed = lax.broadcasted_iota(jnp.int32, wide, 1) == row + lax.rem(me, packed) * slot_rows
    row_slot = lax.div(lax.broadcasted_iota(jnp.int32, (slot_rows, tokens), 0), group).astype(
        jnp.float32
    )
    stat_row = lax.broadcasted_iota(jnp.int32, (STATS, head_dim), 0)

    def owner_group(step, _):
        first = pl.multiple_of(lax.rem(mine + step, groups) * GROUP, GROUP)
        for copy in store_copies(step):
            copy.wait()
        for j in range(GROUP):
            owner = first + j

            @pl.when(owner != me)
            def _():
                ask(me, owner).wait_recv()

        slot_lines = slot_of[pl.ds(first, GROUP), :]
        for j in range(GROUP):
            owner = first + j
            scores = dot_rows(ask_in[owner], store_k[owner]) * factor
            scores = jnp.where(slot_lines[j : j + 1] == row_slot, scores, MASKED)
            weights, lse, inverse = softmax_rows(scores)
            mixed = dot_plain(weights, store_v[owner]) * inverse
            reply_out[owner, pl.ds(0, slot_rows), :] = mixed.astype(jnp.bfloat16)
            line = jnp.sum(jnp.where(placed, lse, 0.0), axis=0, keepdims=True)
            high = line.astype(jnp.bfloat16).astype(jnp.float32)
            middle = (line - high).astype(jnp.bfloat16).astype(jnp.float32)
            low = line - high - middle
            stats = jnp.where(
                stat_row == 0,
                high,
                jnp.where(stat_row == 1, middle, jnp.where(stat_row == 2, low, 0.0)),
            )
            reply_out[owner, pl.ds(slot_rows, STATS), :] = stats.astype(jnp.bfloat16)
        for j in range(GROUP):
            owner = first + j

            @pl.when(owner != me)
            def _():
                reply(owner, me).start()

        return 0

    lax.fori_loop(0, groups, owner_group, 0)
    reply_in[me] = reply_out[me]
    lax.fori_loop(EARLY, requests // BLOCK, local_block, 0)

    def per_row(fresh):
        wide_rows = fresh[...].astype(jnp.float32)[:, None, :]
        return jnp.broadcast_to(wide_rows, (requests, group, head_dim)).reshape(rows, head_dim)

    fresh_score = jnp.sum(
        q_wide[...].reshape(rows, head_dim) * per_row(fresh_k), axis=1, keepdims=True
    )
    fresh_score = fresh_score * factor
    own_lse = local_lse[:, 0:1]

    def settle(step, _):
        other = lax.rem(me + step, helpers)
        reply(me, other).wait_recv()
        return 0

    lax.fori_loop(1, helpers, settle, 0)

    row_index = lax.broadcasted_iota(jnp.int32, (rows, 128), 0)
    parts = []
    highest = jnp.full((rows, 128), MASKED, jnp.float32)
    for part in range(helpers // packed):
        stats = reply_in[pl.ds(part * packed, packed), pl.ds(slot_rows, STATS), :]
        line = jnp.sum(jnp.sum(stats.astype(jnp.float32), axis=0), axis=0, keepdims=True)
        parts.append(line)
        match = row_of[pl.ds(part, 1), :] == row_index
        highest = jnp.maximum(highest, jnp.where(match, line, MASKED))
    peak = jnp.maximum(
        jnp.maximum(fresh_score, own_lse), jnp.max(highest, axis=1, keepdims=True)
    )
    weight_sum = jnp.zeros((rows, 128), jnp.float32)
    fresh_weight = jnp.exp2(fresh_score - peak)
    own_weight = jnp.exp2(own_lse - peak)
    total = fresh_weight * per_row(fresh_v) + own_weight * local_out[...]
    for part in range(helpers // packed):
        match = row_of[pl.ds(part, 1), :] == row_index
        weights = jnp.exp2(jnp.where(match, parts[part], MASKED) - peak)
        weight_sum = weight_sum + weights
        values = reply_in[pl.ds(part * packed, packed), pl.ds(0, slot_rows), :]
        total = total + dot_plain(weights.astype(jnp.bfloat16), values.reshape(128, head_dim))
    denominator = fresh_weight + own_weight + jnp.sum(weight_sum, axis=1, keepdims=True)
    out[...] = (total / denominator).astype(jnp.bfloat16)

    def drain(step, _):
        other = lax.rem(me + step, helpers)
        ask(other, me).wait_send()
        reply(other, me).wait_send()
        return 0

    lax.fori_loop(1, helpers, drain, 0)


def per_device(
    queries,
    new_keys,
    new_values,
    cache_keys,
    cache_values,
    page_table,
    lengths,
    remote_keys,
    remote_values,
    counts,
    page_owner,
    query_list,
):
    requests, group, head_dim = queries.shape
    helpers = lax.axis_size("inst")
    pool, page = cache_keys.shape[:2]
    capacity = remote_keys.shape[0] // helpers
    slots = query_list.shape[2]
    rows, stored = requests * group, capacity * page
    slot_rows = slots * group
    bf16, f32 = jnp.bfloat16, jnp.float32
    smem = pl.BlockSpec(memory_space=pltpu.SMEM)
    vmem = pl.BlockSpec(memory_space=pltpu.VMEM)
    anywhere = pl.BlockSpec(memory_space=pl.ANY)
    attended = pl.pallas_call(
        kernel,
        out_shape=jax.ShapeDtypeStruct((rows, head_dim), bf16),
        in_specs=[smem, smem, smem, vmem, vmem, anywhere, vmem, vmem] + [anywhere] * 4,
        out_specs=vmem,
        scratch_shapes=[
            pltpu.VMEM((rows, head_dim), bf16),
            pltpu.VMEM((requests, group, head_dim), f32),
            pltpu.VMEM((pool, page, head_dim), bf16),
            pltpu.VMEM((pool, page, head_dim), bf16),
            pltpu.VMEM((helpers, stored, head_dim), bf16),
            pltpu.VMEM((helpers, stored, head_dim), bf16),
            pltpu.VMEM((helpers, slot_rows, head_dim), bf16),
            pltpu.VMEM((helpers, slot_rows, head_dim), bf16),
            pltpu.VMEM((helpers, slot_rows + STATS, head_dim), bf16),
            pltpu.VMEM((helpers, slot_rows + STATS, head_dim), bf16),
            pltpu.VMEM((helpers, stored), f32),
            pltpu.VMEM((helpers * slot_rows // 128, 128), jnp.int32),
            pltpu.VMEM((rows, head_dim), f32),
            pltpu.VMEM((rows, head_dim), f32),
            pltpu.SemaphoreType.DMA((3,)),
            pltpu.SemaphoreType.DMA((2, helpers // GROUP)),
            pltpu.SemaphoreType.DMA((helpers,)),
            pltpu.SemaphoreType.DMA((helpers,)),
            pltpu.SemaphoreType.DMA((helpers,)),
            pltpu.SemaphoreType.DMA((helpers,)),
        ],
        compiler_params=pltpu.CompilerParams(
            collective_id=0, has_side_effects=True, vmem_limit_bytes=56 * 1024 * 1024
        ),
        cost_estimate=pl.CostEstimate(
            flops=4 * helpers * slot_rows * stored * head_dim,
            bytes_accessed=24 * helpers * stored * head_dim // 4,
            transcendentals=2 * helpers * slot_rows * stored,
        ),
    )(
        page_table,
        lengths,
        query_list[0].T,
        counts,
        page_owner[0],
        queries.reshape(rows, head_dim),
        new_keys.reshape(requests, head_dim),
        new_values.reshape(requests, head_dim),
        cache_keys.reshape(pool, page, head_dim),
        cache_values.reshape(pool, page, head_dim),
        remote_keys.reshape(helpers, stored, head_dim),
        remote_values.reshape(helpers, stored, head_dim),
    )
    return attended.reshape(requests, group, head_dim)


def solution(mesh):
    return jax.shard_map(
        per_device,
        mesh=mesh,
        in_specs=(
            P("inst", "tp", None),
            P("inst", "tp", None),
            P("inst", "tp", None),
            P("inst", None, "tp", None),
            P("inst", None, "tp", None),
            P("inst", None),
            P("inst"),
            P("inst", None, "tp", None),
            P("inst", None, "tp", None),
            P("inst", None),
            P("inst", None, None),
            P("inst", None, None),
        ),
        out_specs=P("inst", "tp", None),
        check_vma=False,
    )
```

time: 137 us -> 28.9 us (0.21)
  blocking collectives: 71.2 us -> 0 us
  Pallas kernels: 0 us -> 27.2 us
  local copies, waits for them, and re-layouts: 21 us -> 1.47 us
  waiting for transfers between devices: 19.3 us -> 0 us
  matrix products: 14.5 us -> 0 us
  starting transfers between devices: 4.79 us -> 0 us
  other arithmetic: 4.55 us -> 0 us
    all_to_all x2 -> x0, blocking collectives: 71.2 us -> none  [the longest x1 55.6 us: per_device(): lax.all_to_all(remote_keys.reshape(page_block), 'inst', split_axis=0, con...]
    pallas_call x0 -> x1, Pallas kernels: none -> 27.2 us  [per_device(): pl.pallas_call(kernel, out_shape=jax.ShapeDtypeStruct((rows, head_dim), b...]
    all_to_all x1 -> x0, waiting for transfers between devices: 19.3 us -> none  [per_device(): lax.all_to_all(remote_values.reshape(page_block), 'inst', split_axis=0, c...]
    gather x3 -> x0, local copies, waits for them, and re-layouts: 19.3 us -> none  [the longest x1 10.1 us: per_device(): cache_values[page_table]]
    dot_general x8 -> x0, matrix products: 14.5 us -> none  [the longest x1 5.03 us: per_device(): jnp.einsum('aqkgd,atkd->aqkgt', slot_queries, near_keys, preferred_elemen...]
    all_to_all x1 -> x0, starting transfers between devices: 4.79 us -> none  [per_device(): lax.all_to_all(remote_values.reshape(page_block), 'inst', split_axis=0, c...]
    reduce_sum x2 -> x0, other arithmetic: 2.65 us -> none  [partial_softmax(): return (highest, jnp.sum(weights, axis=-1), weights.astype(jnp.bfloat16))]
  transfers between devices with their start and end apart: 1 -> 0, of which waited for: 1 -> 0; matrix products, arithmetic and copies ran while one was open for 24% -> 0% of each run, Pallas kernels for 0% -> 0%
where the time goes in v1:
time: 28.9 us; the launch traced here: 28.7 us
  Pallas kernels  27.2 us (94%)
  local copies, waits for them, and re-layouts  1.47 us (5%)
    pallas_call x1, Pallas kernels, per_device(): pl.pallas_call(kernel, out_shape=jax.ShapeDtypeStruct((rows, head_dim), b...  27.2 us
    unnamed x1, local copies, waits for them, and re-layouts  1.47 us

profile of v1, /device:TPU:1, one launch (start us, length us, event | category | flops | bytes accessed | tf_op | source)
XLA Modules:
  0.0 28.7 jit_solution(7809233028838169553)
XLA Ops:
  0.0 27.2 %shard_map.118 = bf16[256,128]{1,0:T(8,128)(2,1)} custom-call(s32[32,32]{1,0:T(8,128)} %table.1, s32[32]{0:T(128)} %lengths.1, s32[4,32]{1,0:T(4,128)} %bitcast.21, s32[1,32]{1,0:T(1,128)} %counts.1, s32[32,32]{1,0:T(8,128)} %bitcast.18, bf16[256,128]{1,0:T(8,128)(2,1)} %bitcast.17, bf16[32,128]{1,0:T(8,128)(2,1)} %bitcast.19, bf16[32,128]{1,0:T(8,128)(2,1)} %bitcast.20, ...), custom_call_target="tpu_custom_call" | custom-call | flops 268435456 | bytes 12582912 | tf_op jit(solution)/shard_map/pallas_call | solution.py:343
  27.2 1.5 %copy.14 = bf16[32,8,128]{2,1,0:T(8,128)(2,1)} copy(bf16[32,8,128]{2,1,0:T(8,128)(2,1)} %bitcast.16) | data formatting | bytes 131072

commit v2 on v1

--- a/solution.py
+++ b/solution.py
@@ -9,9 +9,12 @@
 from jax.sharding import PartitionSpec as P
 
 MASKED = -1e30
-GROUP = 8
+RING = 4
+CORES = 2
+GROUP = RING * CORES
+FAR_FIRST = (2, 3, 1, 0)
 BLOCK = 4
-EARLY = 4
+EARLY = 8
 STATS = 16
 MESH = pl.DeviceIdType.MESH
 
@@ -32,19 +35,26 @@
 
 
 def kernel(
+    table_hbm,
+    lengths_hbm,
+    lists_hbm,
+    counts_hbm,
+    owners_hbm,
+    q_hbm,
+    fresh_k_hbm,
+    fresh_v_hbm,
+    pool_k_hbm,
+    pool_v_hbm,
+    store_k_hbm,
+    store_v_hbm,
+    out,
     table,
     lengths,
     lists,
     counts,
     owners,
-    q_hbm,
     fresh_k,
     fresh_v,
-    pool_k_hbm,
-    pool_v_hbm,
-    store_k_hbm,
-    store_v_hbm,
-    out,
     q,
     q_wide,
     pool_k,
@@ -59,8 +69,9 @@
     row_of,
     local_out,
     local_lse,
+    score,
+    weight,
     in_sem,
-    store_sem,
     ask_send,
     ask_recv,
     reply_send,
@@ -77,54 +88,99 @@
     groups = helpers // GROUP
     factor = math.log2(math.e) / math.sqrt(head_dim)
     me = lax.axis_index("inst")
-    mine = lax.div(me, GROUP)
+    my_x, my_y, my_core = me // GROUP, me // CORES % RING, me % CORES
+
+    def around(step, sign):
+        x_step = 2 + step - step // 2 * (2 * step - 1)
+        first = (my_x + sign * x_step + RING) % RING * GROUP
+        found = []
+        for y_step in FAR_FIRST:
+            line = first + (my_y + sign * y_step + RING) % RING * CORES
+            for core_step in (1, 0):
+                here = y_step == 0 and core_step == 0
+                found.append((line + (my_core + core_step) % CORES, x_step != 0 if here else None))
+        return found
+
+    def others(step, sign, act):
+        for device, differs in around(step, sign):
+            if differs is None:
+                act(device)
+            else:
+                pl.when(differs)(functools.partial(act, device))
 
     barrier = pltpu.get_barrier_semaphore()
 
     def greet(step, _):
-        pl.semaphore_signal(
-            barrier,
-            inc=1,
-            device_id={"inst": lax.rem(me + step, helpers)},
+        def signal(device):
+            pl.semaphore_signal(
+                barrier, inc=1, device_id={"inst": device}, device_id_type=MESH
+            )
+
+        others(step, 1, signal)
+        return 0
+
+    pairs = (
+        (lists_hbm, lists),
+        (q_hbm, q),
+        (counts_hbm, counts),
+        (owners_hbm, owners),
+        (table_hbm, table),
+        (lengths_hbm, lengths),
+        (pool_k_hbm, pool_k),
+        (pool_v_hbm, pool_v),
+        (store_k_hbm, store_k),
+        (store_v_hbm, store_v),
+        (fresh_k_hbm, fresh_k),
+        (fresh_v_hbm, fresh_v),
+    )
+    copies = [
+        pltpu.make_async_copy(source, target, in_sem.at[n])
+        for n, (source, target) in enumerate(pairs)
+    ]
+    for copy in copies[:6]:
+        copy.start()
+    lax.fori_loop(0, groups, greet, 0)
+    for copy in copies[6:]:
+        copy.start()
+
+    for copy in copies[:2]:
+        copy.wait()
+    q_wide[...] = q[...].astype(jnp.float32).reshape(q_wide.shape)
+
+    def gather(helper, _):
+        picked = [q_wide[lists[slot, helper]] for slot in range(slots)]
+        ask_out[helper] = jnp.concatenate(picked, axis=0).astype(jnp.bfloat16)
+        return 0
+
+    lax.fori_loop(0, helpers, gather, 0)
+    ask_in[me] = ask_out[me]
+    pl.semaphore_wait(barrier, helpers - 1)
+
+    def ask(target, source):
+        return pltpu.make_async_remote_copy(
+            src_ref=ask_out.at[target],
+            dst_ref=ask_in.at[source],
+            send_sem=ask_send.at[target],
+            recv_sem=ask_recv.at[source],
+            device_id={"inst": target},
             device_id_type=MESH,
         )
-        return 0
-
-    q_copy = pltpu.make_async_copy(q_hbm, q, in_sem.at[0])
-    q_copy.start()
-    lax.fori_loop(1, helpers, greet, 0)
-    pool_copies = (
-        pltpu.make_async_copy(pool_k_hbm, pool_k, in_sem.at[1]),
-        pltpu.make_async_copy(pool_v_hbm, pool_v, in_sem.at[2]),
-    )
-    for copy in pool_copies:
-        copy.start()
-
-    def store_copies(step):
-        first = lax.rem(mine + step, groups) * GROUP
-        span = pl.ds(first, GROUP)
-        return (
-            pltpu.make_async_copy(store_k_hbm.at[span], store_k.at[span], store_sem.at[0, step]),
-            pltpu.make_async_copy(store_v_hbm.at[span], store_v.at[span], store_sem.at[1, step]),
+
+    def reply(target, source):
+        return pltpu.make_async_remote_copy(
+            src_ref=reply_out.at[target],
+            dst_ref=reply_in.at[source],
+            send_sem=reply_send.at[target],
+            recv_sem=reply_recv.at[source],
+            device_id={"inst": target},
+            device_id_type=MESH,
         )
 
-    for step in range(groups):
-        for copy in store_copies(step):
-            copy.start()
-
-    square = (helpers, helpers)
-    on_diagonal = lax.broadcasted_iota(jnp.int32, square, 0) == lax.broadcasted_iota(
-        jnp.int32, square, 1
-    )
-    filled = jnp.where(on_diagonal, jnp.broadcast_to(counts[...], square), 0).astype(jnp.float32)
-    filled = jnp.sum(filled, axis=1, keepdims=True)
-    column = lax.broadcasted_iota(jnp.int32, (helpers, capacity), 1).astype(jnp.float32)
-    page_slot = jnp.where(column < filled, owners[...].astype(jnp.float32), -1.0)
-    spread = (
-        lax.div(lax.broadcasted_iota(jnp.int32, (capacity, tokens), 1), page)
-        == lax.broadcasted_iota(jnp.int32, (capacity, tokens), 0)
-    ).astype(jnp.float32)
-    slot_of[...] = dot_plain(page_slot.astype(jnp.bfloat16), spread.astype(jnp.bfloat16))
+    def send_ask(step, _):
+        others(step, 1, lambda device: ask(device, me).start())
+        return 0
+
+    lax.fori_loop(0, groups, send_ask, 0)
 
     lane = lax.broadcasted_iota(jnp.int32, (1, 128), 1)
     packed = 128 // slot_rows
@@ -137,51 +193,25 @@
             )
         row_of[pl.ds(part, 1), :] = line
 
-    q_copy.wait()
-    q_wide[...] = q[...].astype(jnp.float32).reshape(q_wide.shape)
-
-    def gather(helper, _):
-        picked = [q_wide[lists[slot, helper]] for slot in range(slots)]
-        ask_out[helper] = jnp.concatenate(picked, axis=0).astype(jnp.bfloat16)
-        return 0
-
-    lax.fori_loop(0, helpers, gather, 0)
-    ask_in[me] = ask_out[me]
-    pl.semaphore_wait(barrier, helpers - 1)
-
-    def ask(target, source):
-        return pltpu.make_async_remote_copy(
-            src_ref=ask_out.at[target],
-            dst_ref=ask_in.at[source],
-            send_sem=ask_send.at[target],
-            recv_sem=ask_recv.at[source],
-            device_id={"inst": target},
-            device_id_type=MESH,
-        )
-
-    def reply(target, source):
-        return pltpu.make_async_remote_copy(
-            src_ref=reply_out.at[target],
-            dst_ref=reply_in.at[source],
-            send_sem=reply_send.at[target],
-            recv_sem=reply_recv.at[source],
-            device_id={"inst": target},
-            device_id_type=MESH,
-        )
-
-    def send_ask(step, _):
-        first = lax.rem(mine + groups - lax.div(step, GROUP), groups) * GROUP
-        target = first + lax.rem(step, GROUP)
-
-        @pl.when(target != me)
-        def _():
-            ask(target, me).start()
-
-        return 0
-
-    lax.fori_loop(0, helpers, send_ask, 0)
-
-    for copy in pool_copies:
+    for copy in copies[2:4]:
+        copy.wait()
+    square = (helpers, helpers)
+    on_diagonal = lax.broadcasted_iota(jnp.int32, square, 0) == lax.broadcasted_iota(
+        jnp.int32, square, 1
+    )
+    filled = jnp.where(on_diagonal, jnp.broadcast_to(counts[...], square), 0).astype(jnp.float32)
+    filled = jnp.sum(filled, axis=1, keepdims=True)
+    column = lax.broadcasted_iota(jnp.int32, (helpers, capacity), 1).astype(jnp.float32)
+    page_slot = jnp.where(column < filled, owners[...].astype(jnp.float32), -1.0)
+    spread = (
+        lax.div(lax.broadcasted_iota(jnp.int32, (capacity, tokens), 1), page)
+        == lax.broadcasted_iota(jnp.int32, (capacity, tokens), 0)
+    ).astype(jnp.float32)
+    token_slot = dot_plain(page_slot.astype(jnp.bfloat16), spread.astype(jnp.bfloat16))
+    for helper in range(helpers):
+        slot_of[helper] = token_slot[helper : helper + 1]
+
+    for copy in copies[4:8]:
         copy.wait()
     token = lax.broadcasted_iota(jnp.int32, (group, tokens), 1)
 
@@ -223,24 +253,17 @@
     stat_row = lax.broadcasted_iota(jnp.int32, (STATS, head_dim), 0)
 
     def owner_group(step, _):
-        first = pl.multiple_of(lax.rem(mine + step, groups) * GROUP, GROUP)
-        for copy in store_copies(step):
-            copy.wait()
-        for j in range(GROUP):
-            owner = first + j
-
-            @pl.when(owner != me)
-            def _():
-                ask(me, owner).wait_recv()
-
-        slot_lines = slot_of[pl.ds(first, GROUP), :]
-        for j in range(GROUP):
-            owner = first + j
-            scores = dot_rows(ask_in[owner], store_k[owner]) * factor
-            scores = jnp.where(slot_lines[j : j + 1] == row_slot, scores, MASKED)
+        near = [device for device, _ in around(step, -1)]
+        others(step, -1, lambda device: ask(me, device).wait_recv())
+
+        for j, owner in enumerate(near):
+            score[j] = dot_rows(ask_in[owner], store_k[owner])
+        scales = []
+        for j, owner in enumerate(near):
+            scores = jnp.where(slot_of[owner] == row_slot, score[j] * factor, MASKED)
             weights, lse, inverse = softmax_rows(scores)
-            mixed = dot_plain(weights, store_v[owner]) * inverse
-            reply_out[owner, pl.ds(0, slot_rows), :] = mixed.astype(jnp.bfloat16)
+            weight[j] = weights
+            scales.append(inverse)
             line = jnp.sum(jnp.where(placed, lse, 0.0), axis=0, keepdims=True)
             high = line.astype(jnp.bfloat16).astype(jnp.float32)
             middle = (line - high).astype(jnp.bfloat16).astype(jnp.float32)
@@ -251,15 +274,14 @@
                 jnp.where(stat_row == 1, middle, jnp.where(stat_row == 2, low, 0.0)),
             )
             reply_out[owner, pl.ds(slot_rows, STATS), :] = stats.astype(jnp.bfloat16)
-        for j in range(GROUP):
-            owner = first + j
-
-            @pl.when(owner != me)
-            def _():
-                reply(owner, me).start()
-
-        return 0
-
+        for j, owner in enumerate(near):
+            mixed = dot_plain(weight[j], store_v[owner]) * scales[j]
+            reply_out[owner, pl.ds(0, slot_rows), :] = mixed.astype(jnp.bfloat16)
+        others(step, -1, lambda device: reply(device, me).start())
+        return 0
+
+    for copy in copies[8:10]:
+        copy.wait()
     lax.fori_loop(0, groups, owner_group, 0)
     reply_in[me] = reply_out[me]
     lax.fori_loop(EARLY, requests // BLOCK, local_block, 0)
@@ -268,6 +290,9 @@
         wide_rows = fresh[...].astype(jnp.float32)[:, None, :]
         return jnp.broadcast_to(wide_rows, (requests, group, head_dim)).reshape(rows, head_dim)
 
+    for copy in copies[10:]:
+        copy.wait()
+
     fresh_score = jnp.sum(
         q_wide[...].reshape(rows, head_dim) * per_row(fresh_k), axis=1, keepdims=True
     )
@@ -275,11 +300,10 @@
     own_lse = local_lse[:, 0:1]
 
     def settle(step, _):
-        other = lax.rem(me + step, helpers)
-        reply(me, other).wait_recv()
-        return 0
-
-    lax.fori_loop(1, helpers, settle, 0)
+        others(step, 1, lambda device: reply(me, device).wait_recv())
+        return 0
+
+    lax.fori_loop(0, groups, settle, 0)
 
     row_index = lax.broadcasted_iota(jnp.int32, (rows, 128), 0)
     parts = []
@@ -307,12 +331,14 @@
     out[...] = (total / denominator).astype(jnp.bfloat16)
 
     def drain(step, _):
-        other = lax.rem(me + step, helpers)
-        ask(other, me).wait_send()
-        reply(other, me).wait_send()
-        return 0
-
-    lax.fori_loop(1, helpers, drain, 0)
+        def settled(device):
+            ask(device, me).wait_send()
+            reply(device, me).wait_send()
+
+        others(step, 1, settled)
+        return 0
+
+    lax.fori_loop(0, groups, drain, 0)
 
 
 def per_device(
@@ -337,15 +363,21 @@
     rows, stored = requests * group, capacity * page
     slot_rows = slots * group
     bf16, f32 = jnp.bfloat16, jnp.float32
-    smem = pl.BlockSpec(memory_space=pltpu.SMEM)
     vmem = pl.BlockSpec(memory_space=pltpu.VMEM)
     anywhere = pl.BlockSpec(memory_space=pl.ANY)
     attended = pl.pallas_call(
         kernel,
-        out_shape=jax.ShapeDtypeStruct((rows, head_dim), bf16),
-        in_specs=[smem, smem, smem, vmem, vmem, anywhere, vmem, vmem] + [anywhere] * 4,
+        out_shape=pltpu.VMEM((rows, head_dim), bf16),
+        in_specs=[anywhere] * 12,
         out_specs=vmem,
         scratch_shapes=[
+            pltpu.SMEM(page_table.shape, jnp.int32),
+            pltpu.SMEM(lengths.shape, jnp.int32),
+            pltpu.SMEM((slots, helpers), jnp.int32),
+            pltpu.VMEM(counts.shape, jnp.int32),
+            pltpu.VMEM(page_owner.shape[1:], jnp.int32),
+            pltpu.VMEM((requests, head_dim), bf16),
+            pltpu.VMEM((requests, head_dim), bf16),
             pltpu.VMEM((rows, head_dim), bf16),
             pltpu.VMEM((requests, group, head_dim), f32),
             pltpu.VMEM((pool, page, head_dim), bf16),
@@ -356,12 +388,13 @@
             pltpu.VMEM((helpers, slot_rows, head_dim), bf16),
             pltpu.VMEM((helpers, slot_rows + STATS, head_dim), bf16),
             pltpu.VMEM((helpers, slot_rows + STATS, head_dim), bf16),
-            pltpu.VMEM((helpers, stored), f32),
+            pltpu.VMEM((helpers, 1, stored), f32),
             pltpu.VMEM((helpers * slot_rows // 128, 128), jnp.int32),
             pltpu.VMEM((rows, head_dim), f32),
             pltpu.VMEM((rows, head_dim), f32),
-            pltpu.SemaphoreType.DMA((3,)),
-            pltpu.SemaphoreType.DMA((2, helpers // GROUP)),
+            pltpu.VMEM((GROUP, slot_rows, stored), f32),
+            pltpu.VMEM((GROUP, slot_rows, stored), bf16),
+            pltpu.SemaphoreType.DMA((12,)),
             pltpu.SemaphoreType.DMA((helpers,)),
             pltpu.SemaphoreType.DMA((helpers,)),
             pltpu.SemaphoreType.DMA((helpers,)),

time: 28.9 us -> 22.9 us (0.79)
  Pallas kernels: 27.2 us -> 22.1 us
  local copies, waits for them, and re-layouts: 1.47 us -> 0.63 us
    pallas_call x1, Pallas kernels: 27.2 us -> 22.1 us  [per_device(): pl.pallas_call(kernel, out_shape=pltpu.VMEM((rows, head_dim), bf16), in_s...]
    unnamed x1, local copies, waits for them, and re-layouts: 1.47 us -> 0.63 us
where the time goes in v2:
time: 22.9 us; the launch traced here: 22.8 us
  Pallas kernels  22.1 us (97%)
  local copies, waits for them, and re-layouts  0.63 us (3%)
    pallas_call x1, Pallas kernels, per_device(): pl.pallas_call(kernel, out_shape=pltpu.VMEM((rows, head_dim), bf16), in_s...  22.1 us
    unnamed x1, local copies, waits for them, and re-layouts  0.63 us

profile of v2, /device:TPU:1, one launch (start us, length us, event | category | flops | bytes accessed | tf_op | source)
XLA Modules:
  0.0 22.8 jit_solution(926415212788866823)
XLA Ops:
  0.0 22.1 %shard_map.118 = bf16[256,128]{1,0:T(8,128)(2,1)S(1)} custom-call(s32[32,32]{1,0:T(8,128)} %table_hbm.1, s32[32]{0:T(128)} %lengths_hbm.1, s32[4,32]{1,0:T(4,128)} %bitcast.21, s32[1,32]{1,0:T(1,128)} %counts_hbm.1, s32[32,32]{1,0:T(8,128)} %bitcast.18, bf16[256,128]{1,0:T(8,128)(2,1)} %bitcast.17, bf16[32,128]{1,0:T(8,128)(2,1)} %bitcast.19, ...), custom_call_target="tpu_custom_call" | custom-call | flops 268435456 | bytes 12582912 | tf_op jit(solution)/shard_map/pallas_call | solution.py:368
  22.1 0.6 %copy.14 = bf16[32,8,128]{2,1,0:T(8,128)(2,1)} copy(bf16[32,8,128]{2,1,0:T(8,128)(2,1)S(1)} %bitcast.12) | data formatting | bytes 131072

commit v3 on v2

--- a/solution.py
+++ b/solution.py
@@ -11,11 +11,14 @@
 MASKED = -1e30
 RING = 4
 CORES = 2
-GROUP = RING * CORES
-FAR_FIRST = (2, 3, 1, 0)
+GROUP = 8
+STEPS = sorted(
+    ((x, y, core) for x in range(RING) for y in range(RING) for core in range(CORES)),
+    key=lambda at: (-min(at[0], RING - at[0]) - min(at[1], RING - at[1]), -at[2], at),
+)
 BLOCK = 4
-EARLY = 8
-STATS = 16
+CHUNK = 256
+EARLY = 4
 MESH = pl.DeviceIdType.MESH
 
 
@@ -60,20 +63,26 @@
     pool_k,
     pool_v,
     store_k,
+    store_kt,
     store_v,
     ask_out,
     ask_in,
     reply_out,
     reply_in,
+    stat_out,
+    stat_in,
     slot_of,
     row_of,
     local_out,
     local_lse,
     score,
     weight,
+    part_weight,
     in_sem,
     ask_send,
     ask_recv,
+    tell_send,
+    tell_recv,
     reply_send,
     reply_recv,
 ):
@@ -85,39 +94,20 @@
     pages, page = table.shape[1], pool_k.shape[1]
     tokens = pages * page
     capacity = owners.shape[1]
-    groups = helpers // GROUP
     factor = math.log2(math.e) / math.sqrt(head_dim)
     me = lax.axis_index("inst")
-    my_x, my_y, my_core = me // GROUP, me // CORES % RING, me % CORES
-
-    def around(step, sign):
-        x_step = 2 + step - step // 2 * (2 * step - 1)
-        first = (my_x + sign * x_step + RING) % RING * GROUP
-        found = []
-        for y_step in FAR_FIRST:
-            line = first + (my_y + sign * y_step + RING) % RING * CORES
-            for core_step in (1, 0):
-                here = y_step == 0 and core_step == 0
-                found.append((line + (my_core + core_step) % CORES, x_step != 0 if here else None))
-        return found
-
-    def others(step, sign, act):
-        for device, differs in around(step, sign):
-            if differs is None:
-                act(device)
-            else:
-                pl.when(differs)(functools.partial(act, device))
+    my_x = lax.div(me, RING * CORES)
+    my_y = lax.rem(lax.div(me, CORES), RING)
+    my_core = lax.rem(me, CORES)
+    planes = [lax.rem(my_x + step, RING) * (RING * CORES) for step in range(RING)]
+    lines = [lax.rem(my_y + step, RING) * CORES for step in range(RING)]
+    cores = (my_core, CORES - 1 - my_core)
+    ahead = [planes[x] + lines[y] + cores[core] for x, y, core in STEPS]
+    behind = [planes[-x % RING] + lines[-y % RING] + cores[core] for x, y, core in STEPS]
 
     barrier = pltpu.get_barrier_semaphore()
-
-    def greet(step, _):
-        def signal(device):
-            pl.semaphore_signal(
-                barrier, inc=1, device_id={"inst": device}, device_id_type=MESH
-            )
-
-        others(step, 1, signal)
-        return 0
+    for device in ahead[:-1]:
+        pl.semaphore_signal(barrier, inc=1, device_id={"inst": device}, device_id_type=MESH)
 
     pairs = (
         (lists_hbm, lists),
@@ -137,10 +127,7 @@
         pltpu.make_async_copy(source, target, in_sem.at[n])
         for n, (source, target) in enumerate(pairs)
     ]
-    for copy in copies[:6]:
-        copy.start()
-    lax.fori_loop(0, groups, greet, 0)
-    for copy in copies[6:]:
+    for copy in copies:
         copy.start()
 
     for copy in copies[:2]:
@@ -153,41 +140,48 @@
         return 0
 
     lax.fori_loop(0, helpers, gather, 0)
-    ask_in[me] = ask_out[me]
+    ask_in[helpers - 1] = ask_out[me]
     pl.semaphore_wait(barrier, helpers - 1)
 
-    def ask(target, source):
+    def ask(place):
         return pltpu.make_async_remote_copy(
-            src_ref=ask_out.at[target],
-            dst_ref=ask_in.at[source],
-            send_sem=ask_send.at[target],
-            recv_sem=ask_recv.at[source],
-            device_id={"inst": target},
+            src_ref=ask_out.at[ahead[place]],
+            dst_ref=ask_in.at[place],
+            send_sem=ask_send.at[place],
+            recv_sem=ask_recv.at[place],
+            device_id={"inst": ahead[place]},
             device_id_type=MESH,
         )
 
-    def reply(target, source):
+    def answer(place, out_ref, in_ref, send, recv):
         return pltpu.make_async_remote_copy(
-            src_ref=reply_out.at[target],
-            dst_ref=reply_in.at[source],
-            send_sem=reply_send.at[target],
-            recv_sem=reply_recv.at[source],
-            device_id={"inst": target},
+            src_ref=out_ref.at[place],
+            dst_ref=in_ref.at[place],
+            send_sem=send.at[place],
+            recv_sem=recv.at[place],
+            device_id={"inst": behind[place]},
             device_id_type=MESH,
         )
 
-    def send_ask(step, _):
-        others(step, 1, lambda device: ask(device, me).start())
-        return 0
-
-    lax.fori_loop(0, groups, send_ask, 0)
+    def tell(place):
+        return answer(place, stat_out, stat_in, tell_send, tell_recv)
+
+    def reply(place):
+        return answer(place, reply_out, reply_in, reply_send, reply_recv)
+
+    def others(start):
+        return range(start, min(start + GROUP, helpers - 1))
+
+    for place in range(helpers - 1):
+        ask(place).start()
 
     lane = lax.broadcasted_iota(jnp.int32, (1, 128), 1)
     packed = 128 // slot_rows
-    for part in range(helpers // packed):
+    parts = helpers // packed
+    for part in range(parts):
         line = lax.rem(lane, group)
         for piece in range(packed * slots):
-            helper, slot = part * packed + piece // slots, piece % slots
+            helper, slot = ahead[part * packed + piece // slots], piece % slots
             line = jnp.where(
                 lax.div(lane, group) == piece, line + lists[slot, helper] * group, line
             )
@@ -246,44 +240,47 @@
 
     wide = (slot_rows, head_dim)
     row = lax.broadcasted_iota(jnp.int32, wide, 0)
-    placed = lax.broadcasted_iota(jnp.int32, wide, 1) == row + lax.rem(me, packed) * slot_rows
+    offset = lax.broadcasted_iota(jnp.int32, wide, 1) - row
+    placed = [offset == n * slot_rows for n in range(packed)]
     row_slot = lax.div(lax.broadcasted_iota(jnp.int32, (slot_rows, tokens), 0), group).astype(
         jnp.float32
     )
-    stat_row = lax.broadcasted_iota(jnp.int32, (STATS, head_dim), 0)
-
-    def owner_group(step, _):
-        near = [device for device, _ in around(step, -1)]
-        others(step, -1, lambda device: ask(me, device).wait_recv())
-
+
+    def owner_group(start):
+        near = behind[start : start + GROUP]
+        for place in others(start):
+            ask(place).wait_recv()
         for j, owner in enumerate(near):
-            score[j] = dot_rows(ask_in[owner], store_k[owner])
+            score[j] = dot_plain(ask_in[start + j], store_kt[owner])
         scales = []
         for j, owner in enumerate(near):
             scores = jnp.where(slot_of[owner] == row_slot, score[j] * factor, MASKED)
             weights, lse, inverse = softmax_rows(scores)
             weight[j] = weights
             scales.append(inverse)
-            line = jnp.sum(jnp.where(placed, lse, 0.0), axis=0, keepdims=True)
-            high = line.astype(jnp.bfloat16).astype(jnp.float32)
-            middle = (line - high).astype(jnp.bfloat16).astype(jnp.float32)
-            low = line - high - middle
-            stats = jnp.where(
-                stat_row == 0,
-                high,
-                jnp.where(stat_row == 1, middle, jnp.where(stat_row == 2, low, 0.0)),
-            )
-            reply_out[owner, pl.ds(slot_rows, STATS), :] = stats.astype(jnp.bfloat16)
+            line = jnp.where(placed[(start + j) % packed], lse, 0.0)
+            stat_out[start + j] = jnp.sum(line, axis=0, keepdims=True)
+        for place in others(start):
+            tell(place).start()
         for j, owner in enumerate(near):
             mixed = dot_plain(weight[j], store_v[owner]) * scales[j]
-            reply_out[owner, pl.ds(0, slot_rows), :] = mixed.astype(jnp.bfloat16)
-        others(step, -1, lambda device: reply(device, me).start())
-        return 0
+            reply_out[start + j] = mixed.astype(jnp.bfloat16)
+        for place in others(start):
+            reply(place).start()
 
     for copy in copies[8:10]:
         copy.wait()
-    lax.fori_loop(0, groups, owner_group, 0)
-    reply_in[me] = reply_out[me]
+
+    def turn(step, _):
+        for j in range(4):
+            store_kt[4 * step + j] = store_k[4 * step + j].T
+        return 0
+
+    lax.fori_loop(0, helpers // 4, turn, 0)
+    for start in range(0, helpers, GROUP):
+        owner_group(start)
+    reply_in[helpers - 1] = reply_out[helpers - 1]
+    stat_in[helpers - 1] = stat_out[helpers - 1]
     lax.fori_loop(EARLY, requests // BLOCK, local_block, 0)
 
     def per_row(fresh):
@@ -298,47 +295,36 @@
     )
     fresh_score = fresh_score * factor
     own_lse = local_lse[:, 0:1]
-
-    def settle(step, _):
-        others(step, 1, lambda device: reply(me, device).wait_recv())
-        return 0
-
-    lax.fori_loop(0, groups, settle, 0)
-
-    row_index = lax.broadcasted_iota(jnp.int32, (rows, 128), 0)
-    parts = []
-    highest = jnp.full((rows, 128), MASKED, jnp.float32)
-    for part in range(helpers // packed):
-        stats = reply_in[pl.ds(part * packed, packed), pl.ds(slot_rows, STATS), :]
-        line = jnp.sum(jnp.sum(stats.astype(jnp.float32), axis=0), axis=0, keepdims=True)
-        parts.append(line)
-        match = row_of[pl.ds(part, 1), :] == row_index
-        highest = jnp.maximum(highest, jnp.where(match, line, MASKED))
-    peak = jnp.maximum(
-        jnp.maximum(fresh_score, own_lse), jnp.max(highest, axis=1, keepdims=True)
-    )
-    weight_sum = jnp.zeros((rows, 128), jnp.float32)
-    fresh_weight = jnp.exp2(fresh_score - peak)
-    own_weight = jnp.exp2(own_lse - peak)
-    total = fresh_weight * per_row(fresh_v) + own_weight * local_out[...]
-    for part in range(helpers // packed):
-        match = row_of[pl.ds(part, 1), :] == row_index
-        weights = jnp.exp2(jnp.where(match, parts[part], MASKED) - peak)
-        weight_sum = weight_sum + weights
-        values = reply_in[pl.ds(part * packed, packed), pl.ds(0, slot_rows), :]
-        total = total + dot_plain(weights.astype(jnp.bfloat16), values.reshape(128, head_dim))
-    denominator = fresh_weight + own_weight + jnp.sum(weight_sum, axis=1, keepdims=True)
-    out[...] = (total / denominator).astype(jnp.bfloat16)
-
-    def drain(step, _):
-        def settled(device):
-            ask(device, me).wait_send()
-            reply(device, me).wait_send()
-
-        others(step, 1, settled)
-        return 0
-
-    lax.fori_loop(0, groups, drain, 0)
+    fresh_rows = per_row(fresh_v)
+
+    for start in range(0, helpers, GROUP):
+        for place in others(start):
+            tell(place).wait_recv()
+    line = jnp.concatenate(
+        [jnp.sum(stat_in[pl.ds(n * packed, packed)], axis=0) for n in range(parts)], axis=1
+    )
+    owner_row = jnp.concatenate([row_of[pl.ds(n, 1), :] for n in range(parts)], axis=1)
+    for first in range(0, rows, CHUNK):
+        span = slice(first, first + CHUNK)
+        index = lax.broadcasted_iota(jnp.int32, (CHUNK, parts * 128), 0) + first
+        lse = jnp.where(owner_row == index, line, MASKED)
+        own, fresh = own_lse[span], fresh_score[span]
+        peak = jnp.maximum(jnp.maximum(own, fresh), jnp.max(lse, axis=1, keepdims=True))
+        weights = jnp.exp2(lse - peak)
+        part_weight[span, :] = weights.astype(jnp.bfloat16)
+        own, fresh = jnp.exp2(own - peak), jnp.exp2(fresh - peak)
+        inverse = 1.0 / (own + fresh + jnp.sum(weights, axis=1, keepdims=True))
+        local_out[span, :] = (own * local_out[span, :] + fresh * fresh_rows[span]) * inverse
+        local_lse[span, :] = jnp.broadcast_to(inverse, (CHUNK, head_dim))
+    for place in range(helpers - 1):
+        ask(place).wait_send()
+        tell(place).wait_send()
+        reply(place).wait_send()
+    for place in range(helpers - 1):
+        reply(place).wait_recv()
+    values = reply_in[...].reshape(helpers * slot_rows, head_dim)
+    total = dot_plain(part_weight[...], values) * local_lse[...] + local_out[...]
+    out[...] = total.astype(jnp.bfloat16)
 
 
 def per_device(
@@ -383,18 +369,24 @@
             pltpu.VMEM((pool, page, head_dim), bf16),
             pltpu.VMEM((pool, page, head_dim), bf16),
             pltpu.VMEM((helpers, stored, head_dim), bf16),
+            pltpu.VMEM((helpers, head_dim, stored), bf16),
             pltpu.VMEM((helpers, stored, head_dim), bf16),
             pltpu.VMEM((helpers, slot_rows, head_dim), bf16),
             pltpu.VMEM((helpers, slot_rows, head_dim), bf16),
-            pltpu.VMEM((helpers, slot_rows + STATS, head_dim), bf16),
-            pltpu.VMEM((helpers, slot_rows + STATS, head_dim), bf16),
+            pltpu.VMEM((helpers, slot_rows, head_dim), bf16),
+            pltpu.VMEM((helpers, slot_rows, head_dim), bf16),
+            pltpu.VMEM((helpers, 1, 128), f32),
+            pltpu.VMEM((helpers, 1, 128), f32),
             pltpu.VMEM((helpers, 1, stored), f32),
             pltpu.VMEM((helpers * slot_rows // 128, 128), jnp.int32),
             pltpu.VMEM((rows, head_dim), f32),
             pltpu.VMEM((rows, head_dim), f32),
             pltpu.VMEM((GROUP, slot_rows, stored), f32),
             pltpu.VMEM((GROUP, slot_rows, stored), bf16),
+            pltpu.VMEM((rows, helpers * slot_rows), bf16),
             pltpu.SemaphoreType.DMA((12,)),
+            pltpu.SemaphoreType.DMA((helpers,)),
+            pltpu.SemaphoreType.DMA((helpers,)),
             pltpu.SemaphoreType.DMA((helpers,)),
             pltpu.SemaphoreType.DMA((helpers,)),
             pltpu.SemaphoreType.DMA((helpers,)),

time: 22.9 us -> 21.6 us (0.943)
  Pallas kernels: 22.1 us -> 20.9 us
    pallas_call x1, Pallas kernels: 22.1 us -> 20.9 us  [per_device(): pl.pallas_call(kernel, out_shape=pltpu.VMEM((rows, head_dim), bf16), in_s...]
where the time goes in v3:
time: 21.6 us; the launch traced here: 21.5 us
  Pallas kernels  20.9 us (97%)
  local copies, waits for them, and re-layouts  0.63 us (3%)
    pallas_call x1, Pallas kernels, per_device(): pl.pallas_call(kernel, out_shape=pltpu.VMEM((rows, head_dim), bf16), in_s...  20.9 us
    unnamed x1, local copies, waits for them, and re-layouts  0.63 us

profile of v3, /device:TPU:1, one launch (start us, length us, event | category | flops | bytes accessed | tf_op | source)
XLA Modules:
  0.0 21.5 jit_solution(11063419043549814591)
XLA Ops:
  0.0 20.9 %shard_map.118 = bf16[256,128]{1,0:T(8,128)(2,1)S(1)} custom-call(s32[32,32]{1,0:T(8,128)} %table_hbm.1, s32[32]{0:T(128)} %lengths_hbm.1, s32[4,32]{1,0:T(4,128)} %bitcast.21, s32[1,32]{1,0:T(1,128)} %counts_hbm.1, s32[32,32]{1,0:T(8,128)} %bitcast.18, bf16[256,128]{1,0:T(8,128)(2,1)} %bitcast.17, bf16[32,128]{1,0:T(8,128)(2,1)} %bitcast.19, ...), custom_call_target="tpu_custom_call" | custom-call | flops 268435456 | bytes 12582912 | tf_op jit(solution)/shard_map/pallas_call | solution.py:354
  20.9 0.6 %copy.14 = bf16[32,8,128]{2,1,0:T(8,128)(2,1)} copy(bf16[32,8,128]{2,1,0:T(8,128)(2,1)S(1)} %bitcast.12) | data formatting | bytes 131072

commit v4 on v3

--- a/solution.py
+++ b/solution.py
@@ -11,13 +11,12 @@
 MASKED = -1e30
 RING = 4
 CORES = 2
-GROUP = 8
+BOUNDS = (0, 2, 8, 16, 24, 32)
 STEPS = sorted(
     ((x, y, core) for x in range(RING) for y in range(RING) for core in range(CORES)),
     key=lambda at: (-min(at[0], RING - at[0]) - min(at[1], RING - at[1]), -at[2], at),
 )
 BLOCK = 4
-CHUNK = 256
 EARLY = 4
 MESH = pl.DeviceIdType.MESH
 
@@ -169,8 +168,8 @@
     def reply(place):
         return answer(place, reply_out, reply_in, reply_send, reply_recv)
 
-    def others(start):
-        return range(start, min(start + GROUP, helpers - 1))
+    def others(start, stop):
+        return range(start, min(stop, helpers - 1))
 
     for place in range(helpers - 1):
         ask(place).start()
@@ -246,9 +245,9 @@
         jnp.float32
     )
 
-    def owner_group(start):
-        near = behind[start : start + GROUP]
-        for place in others(start):
+    def owner_group(start, stop):
+        near = behind[start:stop]
+        for place in others(start, stop):
             ask(place).wait_recv()
         for j, owner in enumerate(near):
             score[j] = dot_plain(ask_in[start + j], store_kt[owner])
@@ -260,12 +259,12 @@
             scales.append(inverse)
             line = jnp.where(placed[(start + j) % packed], lse, 0.0)
             stat_out[start + j] = jnp.sum(line, axis=0, keepdims=True)
-        for place in others(start):
+        for place in others(start, stop):
             tell(place).start()
         for j, owner in enumerate(near):
             mixed = dot_plain(weight[j], store_v[owner]) * scales[j]
             reply_out[start + j] = mixed.astype(jnp.bfloat16)
-        for place in others(start):
+        for place in others(start, stop):
             reply(place).start()
 
     for copy in copies[8:10]:
@@ -277,8 +276,8 @@
         return 0
 
     lax.fori_loop(0, helpers // 4, turn, 0)
-    for start in range(0, helpers, GROUP):
-        owner_group(start)
+    for start, stop in zip(BOUNDS, BOUNDS[1:]):
+        owner_group(start, stop)
     reply_in[helpers - 1] = reply_out[helpers - 1]
     stat_in[helpers - 1] = stat_out[helpers - 1]
     lax.fori_loop(EARLY, requests // BLOCK, local_block, 0)
@@ -297,25 +296,23 @@
     own_lse = local_lse[:, 0:1]
     fresh_rows = per_row(fresh_v)
 
-    for start in range(0, helpers, GROUP):
-        for place in others(start):
-            tell(place).wait_recv()
+    for place in range(helpers - 1):
+        tell(place).wait_recv()
     line = jnp.concatenate(
         [jnp.sum(stat_in[pl.ds(n * packed, packed)], axis=0) for n in range(parts)], axis=1
     )
     owner_row = jnp.concatenate([row_of[pl.ds(n, 1), :] for n in range(parts)], axis=1)
-    for first in range(0, rows, CHUNK):
-        span = slice(first, first + CHUNK)
-        index = lax.broadcasted_iota(jnp.int32, (CHUNK, parts * 128), 0) + first
-        lse = jnp.where(owner_row == index, line, MASKED)
-        own, fresh = own_lse[span], fresh_score[span]
-        peak = jnp.maximum(jnp.maximum(own, fresh), jnp.max(lse, axis=1, keepdims=True))
-        weights = jnp.exp2(lse - peak)
-        part_weight[span, :] = weights.astype(jnp.bfloat16)
-        own, fresh = jnp.exp2(own - peak), jnp.exp2(fresh - peak)
-        inverse = 1.0 / (own + fresh + jnp.sum(weights, axis=1, keepdims=True))
-        local_out[span, :] = (own * local_out[span, :] + fresh * fresh_rows[span]) * inverse
-        local_lse[span, :] = jnp.broadcast_to(inverse, (CHUNK, head_dim))
+    index = lax.broadcasted_iota(jnp.int32, (rows, parts * 128), 0)
+    lse = jnp.where(owner_row == index, line, MASKED)
+    peak = jnp.maximum(
+        jnp.maximum(own_lse, fresh_score), jnp.max(lse, axis=1, keepdims=True)
+    )
+    weights = jnp.exp2(lse - peak)
+    part_weight[...] = weights.astype(jnp.bfloat16)
+    own, fresh = jnp.exp2(own_lse - peak), jnp.exp2(fresh_score - peak)
+    inverse = 1.0 / (own + fresh + jnp.sum(weights, axis=1, keepdims=True))
+    local_out[...] = (own * local_out[...] + fresh * fresh_rows) * inverse
+    local_lse[...] = jnp.broadcast_to(inverse, (rows, head_dim))
     for place in range(helpers - 1):
         ask(place).wait_send()
         tell(place).wait_send()
@@ -381,8 +378,8 @@
             pltpu.VMEM((helpers * slot_rows // 128, 128), jnp.int32),
             pltpu.VMEM((rows, head_dim), f32),
             pltpu.VMEM((rows, head_dim), f32),
-            pltpu.VMEM((GROUP, slot_rows, stored), f32),
-            pltpu.VMEM((GROUP, slot_rows, stored), bf16),
+            pltpu.VMEM((helpers, slot_rows, stored), f32),
+            pltpu.VMEM((helpers, slot_rows, stored), bf16),
             pltpu.VMEM((rows, helpers * slot_rows), bf16),
             pltpu.SemaphoreType.DMA((12,)),
             pltpu.SemaphoreType.DMA((helpers,)),

time: 21.6 us -> 21.3 us (0.986)
  Pallas kernels: 20.9 us -> 20.5 us
    pallas_call x1, Pallas kernels: 20.9 us -> 20.5 us  [per_device(): pl.pallas_call(kernel, out_shape=pltpu.VMEM((rows, head_dim), bf16), in_s...]
where the time goes in v4:
time: 21.3 us; the launch traced here: 21.2 us
  Pallas kernels  20.5 us (96%)
  local copies, waits for them, and re-layouts  0.63 us (3%)
    pallas_call x1, Pallas kernels, per_device(): pl.pallas_call(kernel, out_shape=pltpu.VMEM((rows, head_dim), bf16), in_s...  20.5 us
    unnamed x1, local copies, waits for them, and re-layouts  0.63 us

profile of v4, /device:TPU:1, one launch (start us, length us, event | category | flops | bytes accessed | tf_op | source)
XLA Modules:
  0.0 21.2 jit_solution(2065189511247643205)
XLA Ops:
  0.0 20.5 %shard_map.118 = bf16[256,128]{1,0:T(8,128)(2,1)S(1)} custom-call(s32[32,32]{1,0:T(8,128)} %table_hbm.1, s32[32]{0:T(128)} %lengths_hbm.1, s32[4,32]{1,0:T(4,128)} %bitcast.21, s32[1,32]{1,0:T(1,128)} %counts_hbm.1, s32[32,32]{1,0:T(8,128)} %bitcast.18, bf16[256,128]{1,0:T(8,128)(2,1)} %bitcast.17, bf16[32,128]{1,0:T(8,128)(2,1)} %bitcast.19, ...), custom_call_target="tpu_custom_call" | custom-call | flops 268435456 | bytes 12582912 | tf_op jit(solution)/shard_map/pallas_call | solution.py:351
  20.5 0.6 %copy.14 = bf16[32,8,128]{2,1,0:T(8,128)(2,1)} copy(bf16[32,8,128]{2,1,0:T(8,128)(2,1)S(1)} %bitcast.12) | data formatting | bytes 131072

commit v5 on v4

--- a/solution.py
+++ b/solution.py
@@ -17,7 +17,7 @@
     key=lambda at: (-min(at[0], RING - at[0]) - min(at[1], RING - at[1]), -at[2], at),
 )
 BLOCK = 4
-EARLY = 4
+EARLY = 3
 MESH = pl.DeviceIdType.MESH
 
 
@@ -259,11 +259,11 @@
             scales.append(inverse)
             line = jnp.where(placed[(start + j) % packed], lse, 0.0)
             stat_out[start + j] = jnp.sum(line, axis=0, keepdims=True)
-        for place in others(start, stop):
-            tell(place).start()
         for j, owner in enumerate(near):
             mixed = dot_plain(weight[j], store_v[owner]) * scales[j]
             reply_out[start + j] = mixed.astype(jnp.bfloat16)
+        for place in others(start, stop):
+            tell(place).start()
         for place in others(start, stop):
             reply(place).start()
 
@@ -281,6 +281,10 @@
     reply_in[helpers - 1] = reply_out[helpers - 1]
     stat_in[helpers - 1] = stat_out[helpers - 1]
     lax.fori_loop(EARLY, requests // BLOCK, local_block, 0)
+    for place in range(helpers - 1):
+        ask(place).wait_send()
+        tell(place).wait_send()
+        reply(place).wait_send()
 
     def per_row(fresh):
         wide_rows = fresh[...].astype(jnp.float32)[:, None, :]
@@ -313,10 +317,6 @@
     inverse = 1.0 / (own + fresh + jnp.sum(weights, axis=1, keepdims=True))
     local_out[...] = (own * local_out[...] + fresh * fresh_rows) * inverse
     local_lse[...] = jnp.broadcast_to(inverse, (rows, head_dim))
-    for place in range(helpers - 1):
-        ask(place).wait_send()
-        tell(place).wait_send()
-        reply(place).wait_send()
     for place in range(helpers - 1):
         reply(place).wait_recv()
     values = reply_in[...].reshape(helpers * slot_rows, head_dim)

time: 21.3 us -> 20.9 us (0.981)
  Pallas kernels: 20.5 us -> 20.1 us
    pallas_call x1, Pallas kernels: 20.5 us -> 20.1 us  [per_device(): pl.pallas_call(kernel, out_shape=pltpu.VMEM((rows, head_dim), bf16), in_s...]
where the time goes in v5:
time: 20.9 us; the launch traced here: 20.8 us
  Pallas kernels  20.1 us (96%)
  local copies, waits for them, and re-layouts  0.63 us (3%)
    pallas_call x1, Pallas kernels, per_device(): pl.pallas_call(kernel, out_shape=pltpu.VMEM((rows, head_dim), bf16), in_s...  20.1 us
    unnamed x1, local copies, waits for them, and re-layouts  0.63 us

profile of v5, /device:TPU:1, one launch (start us, length us, event | category | flops | bytes accessed | tf_op | source)
XLA Modules:
  0.0 20.8 jit_solution(18280264621031796730)
XLA Ops:
  0.0 20.1 %shard_map.118 = bf16[256,128]{1,0:T(8,128)(2,1)S(1)} custom-call(s32[32,32]{1,0:T(8,128)} %table_hbm.1, s32[32]{0:T(128)} %lengths_hbm.1, s32[4,32]{1,0:T(4,128)} %bitcast.21, s32[1,32]{1,0:T(1,128)} %counts_hbm.1, s32[32,32]{1,0:T(8,128)} %bitcast.18, bf16[256,128]{1,0:T(8,128)(2,1)} %bitcast.17, bf16[32,128]{1,0:T(8,128)(2,1)} %bitcast.19, ...), custom_call_target="tpu_custom_call" | custom-call | flops 268435456 | bytes 12582912 | tf_op jit(solution)/shard_map/pallas_call | solution.py:351
  20.1 0.6 %copy.14 = bf16[32,8,128]{2,1,0:T(8,128)(2,1)} copy(bf16[32,8,128]{2,1,0:T(8,128)(2,1)S(1)} %bitcast.12) | data formatting | bytes 131072

commit v6 on v5

--- a/solution.py
+++ b/solution.py
@@ -140,40 +140,6 @@
 
     lax.fori_loop(0, helpers, gather, 0)
     ask_in[helpers - 1] = ask_out[me]
-    pl.semaphore_wait(barrier, helpers - 1)
-
-    def ask(place):
-        return pltpu.make_async_remote_copy(
-            src_ref=ask_out.at[ahead[place]],
-            dst_ref=ask_in.at[place],
-            send_sem=ask_send.at[place],
-            recv_sem=ask_recv.at[place],
-            device_id={"inst": ahead[place]},
-            device_id_type=MESH,
-        )
-
-    def answer(place, out_ref, in_ref, send, recv):
-        return pltpu.make_async_remote_copy(
-            src_ref=out_ref.at[place],
-            dst_ref=in_ref.at[place],
-            send_sem=send.at[place],
-            recv_sem=recv.at[place],
-            device_id={"inst": behind[place]},
-            device_id_type=MESH,
-        )
-
-    def tell(place):
-        return answer(place, stat_out, stat_in, tell_send, tell_recv)
-
-    def reply(place):
-        return answer(place, reply_out, reply_in, reply_send, reply_recv)
-
-    def others(start, stop):
-        return range(start, min(stop, helpers - 1))
-
-    for place in range(helpers - 1):
-        ask(place).start()
-
     lane = lax.broadcasted_iota(jnp.int32, (1, 128), 1)
     packed = 128 // slot_rows
     parts = helpers // packed
@@ -203,6 +169,40 @@
     token_slot = dot_plain(page_slot.astype(jnp.bfloat16), spread.astype(jnp.bfloat16))
     for helper in range(helpers):
         slot_of[helper] = token_slot[helper : helper + 1]
+
+    pl.semaphore_wait(barrier, helpers - 1)
+
+    def ask(place):
+        return pltpu.make_async_remote_copy(
+            src_ref=ask_out.at[ahead[place]],
+            dst_ref=ask_in.at[place],
+            send_sem=ask_send.at[place],
+            recv_sem=ask_recv.at[place],
+            device_id={"inst": ahead[place]},
+            device_id_type=MESH,
+        )
+
+    def answer(place, out_ref, in_ref, send, recv):
+        return pltpu.make_async_remote_copy(
+            src_ref=out_ref.at[place],
+            dst_ref=in_ref.at[place],
+            send_sem=send.at[place],
+            recv_sem=recv.at[place],
+            device_id={"inst": behind[place]},
+            device_id_type=MESH,
+        )
+
+    def tell(place):
+        return answer(place, stat_out, stat_in, tell_send, tell_recv)
+
+    def reply(place):
+        return answer(place, reply_out, reply_in, reply_send, reply_recv)
+
+    def others(start, stop):
+        return range(start, min(stop, helpers - 1))
+
+    for place in range(helpers - 1):
+        ask(place).start()
 
     for copy in copies[4:8]:
         copy.wait()

time: 20.9 us -> 20.8 us (level)
  no operation moved by 1% of the time
where the time goes in v6:
time: 20.8 us; the launch traced here: 20.7 us
  Pallas kernels  20.1 us (97%)
  local copies, waits for them, and re-layouts  0.63 us (3%)
    pallas_call x1, Pallas kernels, per_device(): pl.pallas_call(kernel, out_shape=pltpu.VMEM((rows, head_dim), bf16), in_s...  20.1 us
    unnamed x1, local copies, waits for them, and re-layouts  0.63 us

profile of v6, /device:TPU:1, one launch (start us, length us, event | category | flops | bytes accessed | tf_op | source)
XLA Modules:
  0.0 20.7 jit_solution(14781161790405511978)
XLA Ops:
  0.0 20.1 %shard_map.118 = bf16[256,128]{1,0:T(8,128)(2,1)S(1)} custom-call(s32[32,32]{1,0:T(8,128)} %table_hbm.1, s32[32]{0:T(128)} %lengths_hbm.1, s32[4,32]{1,0:T(4,128)} %bitcast.21, s32[1,32]{1,0:T(1,128)} %counts_hbm.1, s32[32,32]{1,0:T(8,128)} %bitcast.18, bf16[256,128]{1,0:T(8,128)(2,1)} %bitcast.17, bf16[32,128]{1,0:T(8,128)(2,1)} %bitcast.19, ...), custom_call_target="tpu_custom_call" | custom-call | flops 268435456 | bytes 12582912 | tf_op jit(solution)/shard_map/pallas_call | solution.py:351
  20.1 0.6 %copy.14 = bf16[32,8,128]{2,1,0:T(8,128)(2,1)} copy(bf16[32,8,128]{2,1,0:T(8,128)(2,1)S(1)} %bitcast.12) | data formatting | bytes 131072
